TPU v7x, 32 devices: a whole 2x2x4 slice. The times are simulated.
32 devices in a mesh: groups: 2 (over x), gx: 8 (over z, y), gy: 2 (over core).
Axes of the slice: x: 2, y: 2, z: 4, core: 2. Of those that a mesh axis runs over, the one named last changes fastest.
Arguments:
- hidden: bfloat16 [256, 2, 16384], P(('groups', 'gy'), None, 'gx'), parts along dimension 0, may hold values from -60 to 60
- norm_gain: bfloat16 [16384], P('gx'), may hold values from 0.099609375 to 1.8984375
- w_query: bfloat16 [16384, 8192], P('gx', 'gy'), may hold values from -0.5 to 0.5
- key_weight: bfloat16 [16384, 512], P('gx', 'gy'), may hold values from -0.5 to 0.5
- value_weight: bfloat16 [16384, 512], P('gx', 'gy'), may hold values from -0.046875 to 0.046875
- w_out: bfloat16 [8192, 16384], P('gy', 'gx'), may hold values from -0.0625 to 0.0625
- stored_rotated_keys: bfloat16 [256, 1024, 512], P(('groups', 'gx', 'gy')), parts along dimension 0, may hold values from -1240 to 1240
- stored_value_rows: bfloat16 [256, 1024, 512], P(('groups', 'gx', 'gy')), parts along dimension 0, may hold values from -10 to 10
- lengths: int32 [256], P(('groups', 'gx', 'gy')), parts along dimension 0, may hold values from 1 to 1024, 65536 in all
Outputs:
- branch_out: bfloat16 [256, 2, 16384], P(('groups', 'gy'), None, 'gx'), parts along dimension 0
There are 2 independent parts, one for each index of `groups`. A program takes and returns all parts, laid end to end along the dimension named above; an argument that names none is the same for every part. Nothing has to cross between parts.
Inputs may be any that keep to these rules, and one draw needn't show every extreme that they name: Cache positions below a row's length are live; the lengths of one group sum to 65536; some row's length is 1024.
All inputs are finite; a program needn't handle non-finite values.
Results may differ from a plain program's by a relative error of at most 0.008.
Values may be sent and summed in bfloat16 or wider, within the bound.
A program may use at most 128 MiB of HBM per device.

v0:
```python
import math

import jax
import jax.numpy as jnp
from jax import lax
from jax.sharding import PartitionSpec as P

HEAD_SIZE = 128


epsilon = 1e-05
rope_base = 500000.0


def rotary_embed(inputs, token_positions):
    half_dim = inputs.shape[-1] // 2
    frequency = rope_base ** (-jnp.arange(half_dim, dtype=jnp.float32) / half_dim)
    angles = token_positions.astype(jnp.float32)[..., None, None] * frequency
    cosine = jnp.cos(angles)
    sine_part = jnp.sin(angles)
    lower_half = inputs[..., :half_dim]
    upper_half = inputs[..., half_dim:]
    return jnp.concatenate(
        [
            lower_half * cosine - upper_half * sine_part,
            upper_half * cosine + lower_half * sine_part,
        ],
        axis=-1,
    )


def local(
    hidden,
    norm_gain,
    w_query,
    key_weight,
    value_weight,
    w_out,
    stored_rotated_keys,
    stored_value_rows,
    lengths,
):
    gx_count = lax.axis_size("gx")
    gy_count = lax.axis_size("gy")
    local_width = hidden.shape[2]
    full_width = local_width * gx_count
    head_dim = HEAD_SIZE
    local_rows = lengths.shape[0]
    kv_heads = key_weight.shape[1] * gy_count // head_dim
    query_width = w_query.shape[1]
    key_width = key_weight.shape[1]
    gain_wide = norm_gain.astype(jnp.float32)
    inverse = 1.0 / math.sqrt(head_dim)
    cached_key_rows = stored_rotated_keys.reshape(local_rows, -1, kv_heads, head_dim)
    cached_value_rows = stored_value_rows.reshape(local_rows, -1, kv_heads, head_dim)
    live_mask = jnp.arange(cached_key_rows.shape[1])[None, :] < lengths[:, None]
    pieces = []
    key_list = []
    collected_values = []
    for step_index in range(hidden.shape[1]):
        row_block = hidden[:, step_index : step_index + 1]
        project_step_count = row_block.shape[1]
        widened = row_block.astype(jnp.float32)
        partial_sq = jnp.sum(widened * widened, axis=-1)
        row_sumsq = lax.psum(partial_sq, "gx")
        factor = lax.rsqrt(row_sumsq / full_width + epsilon)
        normed = (widened * factor[..., None] * gain_wide).astype(jnp.bfloat16)
        gathered = lax.all_gather(normed, "gy", axis=0, tiled=True)
        flat_rows = gathered.reshape(-1, local_width)
        summed = lax.psum_scatter(
            jnp.concatenate(
                [
                    jnp.dot(flat_rows, w_query, preferred_element_type=jnp.float32),
                    jnp.dot(flat_rows, key_weight, preferred_element_type=jnp.float32),
                    jnp.dot(flat_rows, value_weight, preferred_element_type=jnp.float32),
                ],
                axis=1,
            ),
            "gx",
            scatter_dimension=0,
            tiled=True,
        )
        rounded = summed.astype(jnp.bfloat16)
        mixed = lax.all_to_all(rounded, "gy", split_axis=0, concat_axis=1, tiled=True)
        mixed = mixed.reshape(local_rows, project_step_count, gy_count, -1)
        project_query_rows = mixed[..., :query_width].reshape(
            local_rows, project_step_count, -1, head_dim
        )
        project_fresh_keys = mixed[..., query_width : query_width + key_width].reshape(
            local_rows, project_step_count, -1, head_dim
        )
        project_fresh_values = mixed[..., query_width + key_width :].reshape(
            local_rows, project_step_count, -1, head_dim
        )
        query_rows = project_query_rows
        fresh_keys = project_fresh_keys
        token_positions = lengths[:, None] + step_index + jnp.arange(query_rows.shape[1])
        query_rows, fresh_keys = (
            rotary_embed(query_rows.astype(jnp.float32), token_positions).astype(jnp.bfloat16),
            rotary_embed(fresh_keys.astype(jnp.float32), token_positions).astype(jnp.bfloat16),
        )
        key_list.append(fresh_keys)
        collected_values.append(project_fresh_values)
        attend_fresh_keys = jnp.concatenate(key_list, axis=1)
        attend_step_count = query_rows.shape[1]
        new_count = attend_fresh_keys.shape[1]
        grouped_queries = query_rows.reshape(local_rows, attend_step_count, kv_heads, -1, head_dim)
        score_cache = (
            jnp.einsum(
                "rtgqd,rlgd->rtgql",
                grouped_queries,
                cached_key_rows,
                preferred_element_type=jnp.float32,
            )
            * inverse
        )
        score_cache = jnp.where(live_mask[:, None, None, None, :], score_cache, -jnp.inf)
        score_new = (
            jnp.einsum(
                "rtgqd,rsgd->rtgqs",
                grouped_queries,
                attend_fresh_keys,
                preferred_element_type=jnp.float32,
            )
            * inverse
        )
        visible = (
            jnp.arange(new_count)[None, :] <= (step_index + jnp.arange(attend_step_count))[:, None]
        )
        score_new = jnp.where(visible[None, :, None, None, :], score_new, -jnp.inf)
        highest = jnp.maximum(jnp.max(score_cache, axis=-1), jnp.max(score_new, axis=-1))
        exp_cache = jnp.exp(score_cache - highest[..., None])
        exp_new = jnp.exp(score_new - highest[..., None])
        denominator = jnp.sum(exp_cache, axis=-1) + jnp.sum(exp_new, axis=-1)
        weight_cache = (exp_cache / denominator[..., None]).astype(jnp.bfloat16)
        weight_new = (exp_new / denominator[..., None]).astype(jnp.bfloat16)
        attend_attended = jnp.einsum(
            "rtgql,rlgd->rtgqd", weight_cache, cached_value_rows, preferred_element_type=jnp.float32
        )
        attend_attended = attend_attended + jnp.einsum(
            "rtgqs,rsgd->rtgqd",
            weight_new,
            jnp.concatenate(collected_values, axis=1),
            preferred_element_type=jnp.float32,
        )
        attended = attend_attended.astype(jnp.bfloat16)
        step_count = attended.shape[1]
        blocks = attended.reshape(local_rows * step_count, gy_count, -1)
        returned = lax.all_to_all(blocks, "gy", split_axis=1, concat_axis=0, tiled=True).reshape(
            -1, blocks.shape[2]
        )
        out_terms = jnp.dot(
            lax.all_gather(returned, "gx", axis=0, tiled=True),
            w_out,
            preferred_element_type=jnp.float32,
        )
        reduced = lax.psum_scatter(out_terms, "gy", scatter_dimension=0, tiled=True)
        pieces.append(reduced.astype(jnp.bfloat16).reshape(-1, step_count, local_width))
    result = jnp.concatenate(pieces, axis=1)
    return result


def solution(mesh):
    return jax.shard_map(
        local,
        mesh=mesh,
        in_specs=(
            P(("groups", "gy"), None, "gx"),
            P("gx"),
            P("gx", "gy"),
            P("gx", "gy"),
            P("gx", "gy"),
            P("gy", "gx"),
            P(("groups", "gx", "gy"), None, None),
            P(("groups", "gx", "gy"), None, None),
            P(("groups", "gx", "gy")),
        ),
        out_specs=P(("groups", "gy"), None, "gx"),
        check_vma=False,
    )
```

profile of v0, /device:TPU:0, one launch (start us, length us, event | category | flops | bytes accessed | tf_op | source)
XLA Modules:
  0.0 318.9 jit_solution(17999129115103358730)
XLA Ops:
  6.5 0.8 convert_element_type.156
  7.3 2.2 fusion.92
  9.5 0.4 fusion.48
  9.9 23.3 %all-reduce = (f32[64,1]{0,1:T(1,128)S(1)}, f32[64,1]{0,1:T(1,128)S(1)}) all-reduce(f32[64,1]{0,1:T(1,128)S(1)} %bitcast.234, f32[64,1]{0,1:T(1,128)S(1)} %bitcast.233), channel_id=1, replica_groups=mesh['groups'=2,'gx'=8,'gy'=2] {'gx'}, use_global_device_ids=true, to_apply=%region_7.8 | all-reduce | flops 128 | bytes 1024 | tf_op jit(solution)/shard_map/psum | solution.py:65
  33.1 0.4 fusion.50
  33.6 2.2 all_gather.12
  35.8 0.3 fusion.62
  36.1 0.3 fusion.60
  36.4 8.1 %fusion.64 = f32[128,4096]{1,0:T(8,128)S(1)} fusion(bf16[2048,4096]{1,0:T(8,128)(2,1)} %param.11, bf16[128,1,2048]{2,0,1:T(8,128)(2,1)S(1)} %all_gather.12), kind=kOutput, calls=%fused_computation.69 | convolution fusion | flops 2147483648 | bytes 19398656 | tf_op jit(solution)/shard_map/dot_general | solution.py:73
  44.6 1.6 pad_maximum_fusion
  46.3 2.2 all_gather.14
  48.4 0.3 fusion.56
  48.8 0.3 fusion.54
  49.1 8.4 %fusion.58 = f32[128,4096]{1,0:T(8,128)S(1)} fusion(bf16[2048,4096]{1,0:T(8,128)(2,1)} %param.11, bf16[128,1,2048]{2,0,1:T(8,128)(2,1)S(1)} %all_gather.14), kind=kOutput, calls=%fused_computation.63 | convolution fusion | flops 2147483648 | bytes 19398656 | tf_op jit(solution)/shard_map/dot_general | solution.py:73
  57.4 1.6 pad_maximum_fusion.1
  59.1 0.6 copy-done.3
  59.8 0.1 multiply_cosine_fusion.1
  59.9 52.7 %reduce-scatter.5.cloned.1.call-done = f32[16,4608]{1,0:T(8,128)} async-done(((f32[128,4608]{1,0:T(8,128)}), f32[16,4608]{1,0:T(8,128)}) %reduce-scatter.5.cloned.1.call-update) | async-done | bytes 294928 | tf_op jit(solution)/shard_map/reduce_scatter | solution.py:70
  112.6 1.0 convert_bitcast_fusion.3
  113.6 3.8 %all_to_all.62 = bf16[2,8,4608]{2,1,0:T(8,128)(2,1)S(1)} all-to-all(bf16[2,8,4608]{2,1,0:T(8,128)(2,1)S(1)} %convert_bitcast_fusion.3), channel_id=1, replica_groups=mesh['groups'=2,'gx'=8,'gy'=2] {'gy'}, dimensions={0} | all-to-all | bytes 294912 | tf_op jit(solution)/shard_map/all_to_all | solution.py:84
  117.4 66.6 %reduce-scatter.9.cloned.1.call-done = f32[16,4608]{1,0:T(8,128)} async-done(((f32[128,4608]{1,0:T(8,128)}), f32[16,4608]{1,0:T(8,128)}) %reduce-scatter.9.cloned.1.call-update) | async-done | bytes 294928 | tf_op jit(solution)/shard_map/reduce_scatter | solution.py:70
  184.0 1.0 convert_bitcast_fusion.2
  185.0 3.8 %all_to_all.63 = bf16[2,8,4608]{2,1,0:T(8,128)(2,1)S(1)} all-to-all(bf16[2,8,4608]{2,1,0:T(8,128)(2,1)S(1)} %convert_bitcast_fusion.2), channel_id=1, replica_groups=mesh['groups'=2,'gx'=8,'gy'=2] {'gy'}, dimensions={0} | all-to-all | bytes 294912 | tf_op jit(solution)/shard_map/all_to_all | solution.py:84
  188.8 0.2 copy.61
  189.1 0.2 reshape.529
  189.5 0.2 copy.52
  189.7 0.2 reshape.526
  190.0 0.2 subtract_convert_fusion.1
  190.2 0.2 fusion.66
  190.5 5.9 %fusion.16 = (f32[8,4,16]{2,1,0:T(4,128)S(1)}, f32[8,4,16,1024]{3,2,1,0:T(8,128)S(1)}) fusion(pred[8,1024]{1,0:T(8,128)(4,1)S(1)} %iota_compare_fusion, bf16[8,4,16,64]{3,2,1,0:T(8,128)(2,1)S(1)} %bitcast.218, bf16[8,4,16,64]{3,2,1,0:T(8,128)(2,1)S(1)} %bitcast.216, bf16[8,1024,512]{2,1,0:T(8,128)(2,1)} %param.15), kind=kOutput, calls=%fused_computation.24 | convolution fusion | flops 136052224 | bytes 10627072 | tf_op jit(solution)/shard_map/rtgqd,rlgd->rtgql/dot_general | solution.py:109
  196.4 0.2 subtract_convert_fusion
  196.6 5.1 %fusion.14 = (f32[8,4,16]{2,1,0:T(4,128)S(1)}, f32[8,4,16]{2,1,0:T(4,128)S(1)}, f32[8,4,16,1024]{3,2,1,0:T(8,128)S(1)}) fusion(f32[8,4,16,1024]{3,2,1,0:T(8,128)S(1)} %get-tuple-element.37, f32[8,4,16]{2,1,0:T(4,128)S(1)} %multiply_maximum_fusion, pred[8,1024]{1,0:T(8,128)(4,1)S(1)} %iota_compare_fusion, bf16[8,4,16,64]{3,2,1,0:T(8,128)(2,1)S(1)} %bitcast.229, ...), kind=kOutput, calls=%fused_computation.22 | convolution fusion | flops 138148864 | bytes 12728320 | tf_op jit(solution)/shard_map/rtgqd,rlgd->rtgql/dot_general | solution.py:109
  201.8 1.5 fusion.32
  203.4 4.5 %all_to_all.64 = bf16[8,2,4096]{2,0,1:T(8,128)(2,1)} all-to-all(bf16[8,2,4096]{2,0,1:T(8,128)(2,1)S(1)} %copy.59), channel_id=1, replica_groups=mesh['groups'=2,'gx'=8,'gy'=2] {'gy'}, dimensions={1} | all-to-all | bytes 262144 | tf_op jit(solution)/shard_map/all_to_all | solution.py:149
  208.3 0.3 fusion.95
  208.7 0.6 fusion.15
  209.3 4.3 %fusion.21 = f32[8,4,128,16]{2,3,1,0:T(8,128)S(1)} fusion(f32[8,4,16,1024]{3,2,1,0:T(8,128)S(1)} %get-tuple-element.38, f32[8,4,16]{2,1,0:T(4,128)S(1)} %add.70, f32[8,4,16]{2,1,0:T(4,128)S(1)} %max.18, pred[8,1024]{1,0:T(8,128)(4,1)S(1)} %iota_compare_fusion, bf16[8,1024,512]{2,1,0:T(8,128)(2,1)} %param.16), kind=kOutput, calls=%fused_computation.28 | convolution fusion | flops 136839168 | bytes 10760192 | tf_op jit(solution)/shard_map/rtgql,rlgd->rtgqd/dot_general | solution.py:137
  213.6 0.2 fusion.31
  213.9 4.5 %all_to_all.65 = bf16[8,2,4096]{2,0,1:T(8,128)(2,1)} all-to-all(bf16[8,2,4096]{2,0,1:T(8,128)(2,1)S(1)} %copy.69), channel_id=1, replica_groups=mesh['groups'=2,'gx'=8,'gy'=2] {'gy'}, dimensions={1} | all-to-all | bytes 262144 | tf_op jit(solution)/shard_map/all_to_all | solution.py:149
  218.5 28.8 %all-gather.3.cloned.1.call-done = bf16[128,4096]{1,0:T(8,128)(2,1)} async-done(((bf16[16,4096]{1,0:T(8,128)(2,1)}), bf16[128,4096]{1,0:T(8,128)(2,1)}) %all-gather.3.cloned.1.call-update) | async-done | bytes 1048592 | tf_op jit(solution)/shard_map/all_gather | solution.py:153
  247.3 9.5 %fusion.96 = f32[128,2048]{1,0:T(8,128)} fusion(bf16[128,4096]{1,0:T(8,128)(2,1)} %all-gather.3.cloned.1.call-done, bf16[4096,2048]{1,0:T(8,128)(2,1)} %param.14), kind=kOutput, calls=%fused_computation.138 | convolution fusion | flops 2147483648 | bytes 18874368 | tf_op jit(solution)/shard_map/dot_general | solution.py:152
  256.8 0.3 reduce-scatter.11.cloned.1.call-start
  257.1 31.2 %all-gather.5.cloned.1.call-done = bf16[128,4096]{1,0:T(8,128)(2,1)} async-done(((bf16[16,4096]{1,0:T(8,128)(2,1)}), bf16[128,4096]{1,0:T(8,128)(2,1)}) %all-gather.5.cloned.1.call-update) | async-done | bytes 1048592 | tf_op jit(solution)/shard_map/all_gather | solution.py:153
  288.2 9.4 %fusion.97 = f32[128,2048]{1,0:T(8,128)} fusion(bf16[128,4096]{1,0:T(8,128)(2,1)} %all-gather.5.cloned.1.call-done, bf16[4096,2048]{1,0:T(8,128)(2,1)} %param.14), kind=kOutput, calls=%fused_computation.139 | convolution fusion | flops 2147483648 | bytes 18874368 | tf_op jit(solution)/shard_map/dot_general | solution.py:152
  297.7 1.2 convert_bitcast_fusion.1
  298.9 10.7 %reduce-scatter.11.cloned.1.call-done = f32[64,2048]{1,0:T(8,128)} async-done(((f32[128,2048]{1,0:T(8,128)}), f32[64,2048]{1,0:T(8,128)}) %reduce-scatter.11.cloned.1.call-update) | async-done | bytes 524304 | tf_op jit(solution)/shard_map/reduce_scatter | solution.py:157
  309.6 1.1 convert_bitcast_fusion
  310.7 1.3 copy.70
  (59 shorter events, 1.3 us)
Async XLA Ops:
  6.5 29.2 %copy-start = (bf16[2048,256]{1,0:T(8,128)(2,1)S(1)}, bf16[2048,256]{1,0:T(8,128)(2,1)}, u32[]{:S(2)}) copy-start(bf16[2048,256]{1,0:T(8,128)(2,1)} %param.12) | copy-start | bytes 3145732
  6.5 106.0 %reduce-scatter.5.cloned.1.call-start = ((), (), s32[]{:S(2)}) async-start(), calls=%async_computation.8 | async-start | bytes 2654208 | tf_op jit(solution)/shard_map/reduce_scatter | solution.py:70
  9.9 26.2 %copy-start.2 = (bf16[2048,256]{1,0:T(8,128)(2,1)S(1)}, bf16[2048,256]{1,0:T(8,128)(2,1)}, u32[]{:S(2)}) copy-start(bf16[2048,256]{1,0:T(8,128)(2,1)} %param.13) | copy-start | bytes 3145732
  46.2 137.8 %reduce-scatter.9.cloned.1.call-start = ((), (), s32[]{:S(2)}) async-start(), calls=%async_computation.11 | async-start | bytes 2654208 | tf_op jit(solution)/shard_map/reduce_scatter | solution.py:70
  59.0 0.7 copy-start.3
  59.1 188.3 %all-gather.3.cloned.1.call-start = ((), (), s32[]{:S(2)}) async-start(), calls=%async_computation.9 | async-start | bytes 1179648 | tf_op jit(solution)/shard_map/all_gather | solution.py:153
  190.5 11.3 %slice-start = ((s8[8388608]{0:T(1024)(128)(4,1)}), s8[4194304]{0:T(1024)(128)(4,1)S(1)}, s32[]{:S(2)}) async-start(s8[8388608]{0:T(1024)(128)(4,1)} %bitcast.235), calls=%async_computation.14 | async-start | bytes 8388608
  196.6 5.2 %slice-start.1 = ((s8[8388608]{0:T(1024)(128)(4,1)}), s8[4194304]{0:T(1024)(128)(4,1)S(1)}, s32[]{:S(2)}) async-start(s8[8388608]{0:T(1024)(128)(4,1)} %bitcast.235), calls=%async_computation.15 | async-start | bytes 8388608
  208.0 80.3 %all-gather.5.cloned.1.call-start = ((), (), s32[]{:S(2)}) async-start(), calls=%async_computation.12 | async-start | bytes 1179648 | tf_op jit(solution)/shard_map/all_gather | solution.py:153
  218.5 79.3 %reduce-scatter.7.cloned.1.call-start = ((), (), s32[]{:S(2)}) async-start(), calls=%async_computation.10 | async-start | bytes 1572864 | tf_op jit(solution)/shard_map/reduce_scatter | solution.py:157
  256.8 52.8 %reduce-scatter.11.cloned.1.call-start = ((), (), s32[]{:S(2)}) async-start(), calls=%async_computation.13 | async-start | bytes 1572864 | tf_op jit(solution)/shard_map/reduce_scatter | solution.py:157
  297.7 14.3 %copy-start.1 = (bf16[2048,256]{1,0:T(8,128)(2,1)S(1)}, bf16[2048,256]{1,0:T(8,128)(2,1)}, u32[]{:S(2)}) copy-start(bf16[2048,256]{1,0:T(8,128)(2,1)} %param.12) | copy-start | bytes 3145732
Sparse Core Ops, SparseCore 0:
  46.3 66.2 reduce-scatter.4
  116.1 67.8 reduce-scatter.8
  208.1 39.1 all-gather.2
  249.3 38.8 all-gather.4
  290.3 7.2 reduce-scatter.6
  299.8 9.6 reduce-scatter.10
where the time goes:
time: 319 us
  waiting for transfers between devices  190 us (60%)
  matrix products  54.3 us (17%)
  blocking collectives  44.3 us (14%)
  between operations  13.9 us (4%)
  other arithmetic  10.6 us (3%)
  local copies, waits for them, and re-layouts  5.35 us (2%)
    reduce_scatter x2, waiting for transfers between devices, local(): lax.psum_scatter(jnp.concatenate([jnp.dot(flat_rows, w_query, preferred_e...  119 us
    all_gather x2, waiting for transfers between devices, local(): lax.all_gather(returned, 'gx', axis=0, tiled=True)  60 us
    psum x1, blocking collectives, local(): row_sumsq = lax.psum(partial_sq, 'gx')  23.3 us
    dot_general x2, matrix products, local(): jnp.dot(lax.all_gather(returned, 'gx', axis=0, tiled=True), w_out, prefer...  18.9 us
    dot_general x2, matrix products, local(): jnp.dot(flat_rows, w_query, preferred_element_type=jnp.float32)  16.5 us
    dot_general x2, matrix products, local(): jnp.einsum('rtgqd,rlgd->rtgql', grouped_queries, cached_key_rows, preferr...  11 us
    reduce_scatter x2, waiting for transfers between devices, local(): reduced = lax.psum_scatter(out_terms, 'gy', scatter_dimension=0, tiled=True)  10.7 us
    all_to_all x2, blocking collectives, local(): lax.all_to_all(blocks, 'gy', split_axis=1, concat_axis=0, tiled=True)  9.06 us
  transfers between devices with their start and end apart: 6, of which 5 were waited for; matrix products, arithmetic and copies ran while one was open for 12% of the time, Pallas kernels for 0%

commit v1 on v0

v1 whole, which is shorter than its diff:
```python
import functools
import math

import jax
import jax.numpy as jnp
from jax import lax
from jax.experimental import pallas as pl
from jax.experimental.pallas import tpu as pltpu
from jax.sharding import PartitionSpec as P

HEAD_SIZE = 128
CHUNK = 512
WIRE = jnp.int16
SMALL = 2.0**-20
CODES = 32767.0 / math.log(2.0**34.5)
epsilon = 1e-05
rope_base = 500000.0


def encode(values):
    size = jnp.log(1.0 + jnp.abs(values) * (1.0 / SMALL)) * CODES + 0.5
    return jnp.where(values < 0, -size, size).astype(jnp.int32).astype(WIRE)


def decode(codes):
    wide = codes.astype(jnp.int32).astype(jnp.float32)
    size = jnp.exp(jnp.abs(wide) * (1.0 / CODES)) * SMALL - SMALL
    return jnp.where(wide < 0, -size, size)


def remote(src, dst, send, recv, device):
    return pltpu.make_async_remote_copy(
        src_ref=src,
        dst_ref=dst,
        send_sem=send,
        recv_sem=recv,
        device_id=device,
        device_id_type=pl.DeviceIdType.MESH,
    )


def position(gx_count):
    gx = lax.axis_index("gx")
    core = lax.axis_index("gy")
    depth = gx_count // 2
    far, near = gx // 2, lax.rem(gx, 2)
    sibling = {"gy": 1 - core}
    pair = {"gx": far * 2 + (1 - near)}

    def line(d):
        return {"gx": lax.rem(far + d, depth) * 2 + near}

    return core, far, near, sibling, pair, line


def greet(sibling, pair, line, depth):
    barrier = pltpu.get_barrier_semaphore()
    devices = [sibling, pair] + [line(d) for d in range(1, depth)]
    for device in devices:
        pl.semaphore_signal(
            barrier, inc=1, device_id=device, device_id_type=pl.DeviceIdType.MESH
        )
    pl.semaphore_wait(barrier, len(devices))


def project_kernel(
    gx_count,
    rows_block,
    x_ref,
    gain_ref,
    wq_ref,
    kw_ref,
    vw_ref,
    out_ref,
    wbuf,
    xs,
    mine,
    mid,
    pair_sums,
    line_sums,
    normed,
    own,
    s1,
    r1,
    s2,
    r2,
    fin,
    fin_in,
    wsem,
    xsem,
    psem,
    lsem,
    s1s,
    s1r,
    s2s,
    s2r,
    fsem,
):
    depth = gx_count // 2
    chunks, width, _ = wbuf.shape
    half_rows = xs.shape[1]
    rows = 2 * half_rows
    key_width = kw_ref.shape[1]
    core, far, near, sibling, pair, line = position(gx_count)

    def load_query(c):
        return pltpu.make_async_copy(
            wq_ref.at[:, pl.ds(pl.multiple_of(c * CHUNK, CHUNK), CHUNK)],
            wbuf.at[c],
            wsem.at[c],
        )

    load_key = pltpu.make_async_copy(
        kw_ref, wbuf.at[chunks - 1, :, pl.ds(0, key_width)], wsem.at[chunks - 1]
    )
    load_value = pltpu.make_async_copy(
        vw_ref, wbuf.at[chunks - 1, :, pl.ds(key_width, key_width)], wsem.at[chunks]
    )

    @pl.loop(0, chunks - 1)
    def _(c):
        load_query(c).start()

    load_key.start()
    load_value.start()
    greet(sibling, pair, line, depth)

    send_x = remote(x_ref, xs.at[core], xsem.at[0], xsem.at[1], sibling)
    send_x.start()
    xs[core] = x_ref[...]
    send_x.wait()

    columns = []
    for g in range(2):
        wide = xs[g].astype(jnp.float32)
        columns.append(jnp.sum(wide * wide, axis=1, keepdims=True))
    column = jnp.concatenate(columns, axis=0)
    mine[...] = jnp.transpose(jnp.broadcast_to(column, (rows, 128)))[0:8, :]
    swap = remote(mine, pair_sums, psem.at[0], psem.at[1], pair)
    swap.start()
    swap.wait()
    mid[...] = mine[...] + pair_sums[...]
    line_copies = [
        remote(mid, line_sums.at[d], lsem.at[0, d], lsem.at[1, d], line(d))
        for d in range(1, depth)
    ]
    for copy in line_copies:
        copy.start()
    for copy in line_copies:
        copy.wait()
    total = mid[...]
    for d in range(1, depth):
        total = total + line_sums[d]
    factor_row = lax.rsqrt(total * (1.0 / (width * gx_count)) + epsilon)
    factor = jnp.transpose(jnp.broadcast_to(factor_row[0:1, :], (128, rows)))[:, 0:1]
    gain = gain_ref[...].astype(jnp.float32)
    blocks_half = half_rows // rows_block
    for b in range(2 * blocks_half):
        start = (b % blocks_half) * rows_block
        wide = xs[b // blocks_half, start : start + rows_block, :].astype(jnp.float32)
        scaled = wide * factor[b * rows_block : (b + 1) * rows_block, :] * gain
        normed[(b % 2) * depth + b // 2] = scaled.astype(jnp.bfloat16)

    def first(c):
        return remote(s1.at[c], r1.at[c], s1s.at[c], s1r.at[c], pair)

    def second(c, d):
        return remote(
            s2.at[c, lax.rem(far + d, depth)], r2.at[c, d], s2s.at[c, d], s2r.at[c, d], line(d)
        )

    lag = 2

    @pl.loop(0, chunks + lag)
    def _(c):
        @pl.when(c < chunks)
        def _():
            @pl.when(c < chunks - 1)
            def _():
                load_query(c).wait()

            @pl.when(c == chunks - 1)
            def _():
                load_key.wait()
                load_value.wait()

            part = jnp.dot(
                normed[...].reshape(rows, width), wbuf[c], preferred_element_type=jnp.float32
            ).reshape(2, depth, rows_block, CHUNK)

            @pl.when(near == 0)
            def _():
                own[c] = part[0]
                s1[c] = encode(part[1])

            @pl.when(near == 1)
            def _():
                own[c] = part[1]
                s1[c] = encode(part[0])

            first(c).start()

        @pl.when(c >= lag)
        def _():
            cc = c - lag
            first(cc).wait_recv()
            both = own[cc] + decode(r1[cc])
            own[cc] = both
            s2[cc] = encode(both)
            for d in range(1, depth):
                second(cc, d).start()

    @pl.loop(0, chunks)
    def _(c):
        summed = own[c, far]
        for d in range(1, depth):
            second(c, d).wait_recv()
            summed = summed + decode(r2[c, d])
        rounded = summed.astype(jnp.bfloat16)
        for g in range(2):
            fin[g, c] = rounded[g * (rows_block // 2) : (g + 1) * (rows_block // 2), :]

    last = remote(fin.at[1 - core], fin_in, fsem.at[0], fsem.at[1], sibling)
    last.start()
    out_ref[core] = fin[core]

    @pl.loop(0, chunks)
    def _(c):
        first(c).wait_send()
        for d in range(1, depth):
            second(c, d).wait_send()

    last.wait()
    out_ref[1 - core] = fin_in[...]


def project(x, gain, w_query, key_weight, value_weight, gx_count):
    half_rows, width = x.shape
    rows = 2 * half_rows
    rows_block = rows // gx_count
    depth = gx_count // 2
    chunks = w_query.shape[1] // CHUNK + 1
    out_rows = rows_block // 2
    vmem = pl.BlockSpec(memory_space=pltpu.VMEM)
    hbm = pl.BlockSpec(memory_space=pl.ANY)
    dma = pltpu.SemaphoreType.DMA
    return pl.pallas_call(
        functools.partial(project_kernel, gx_count, rows_block),
        out_shape=jax.ShapeDtypeStruct((2, chunks, out_rows, CHUNK), jnp.bfloat16),
        in_specs=[vmem, vmem, hbm, hbm, hbm],
        out_specs=vmem,
        scratch_shapes=[
            pltpu.VMEM((chunks, width, CHUNK), jnp.bfloat16),
            pltpu.VMEM((2, half_rows, width), jnp.bfloat16),
            pltpu.VMEM((8, rows), jnp.float32),
            pltpu.VMEM((8, rows), jnp.float32),
            pltpu.VMEM((8, rows), jnp.float32),
            pltpu.VMEM((depth, 8, rows), jnp.float32),
            pltpu.VMEM((2 * depth, rows_block, width), jnp.bfloat16),
            pltpu.VMEM((chunks, depth, rows_block, CHUNK), jnp.float32),
            pltpu.VMEM((chunks, depth, rows_block, CHUNK), WIRE),
            pltpu.VMEM((chunks, depth, rows_block, CHUNK), WIRE),
            pltpu.VMEM((chunks, depth, rows_block, CHUNK), WIRE),
            pltpu.VMEM((chunks, depth, rows_block, CHUNK), WIRE),
            pltpu.VMEM((2, chunks, out_rows, CHUNK), jnp.bfloat16),
            pltpu.VMEM((chunks, out_rows, CHUNK), jnp.bfloat16),
            dma((chunks + 1,)),
            dma((2,)),
            dma((2,)),
            dma((2, depth)),
            dma((chunks,)),
            dma((chunks,)),
            dma((chunks, depth)),
            dma((chunks, depth)),
            dma((2,)),
        ],
        compiler_params=pltpu.CompilerParams(
            collective_id=1, has_side_effects=True, vmem_limit_bytes=56 * 1024 * 1024
        ),
    )(x, gain, w_query, key_weight, value_weight)


def output_kernel(
    gx_count,
    att_ref,
    w_ref,
    out_ref,
    wbuf,
    full,
    acc,
    acc_in,
    wsem,
    gsem,
    zs,
    zr,
    ys,
    yr,
    fsem,
):
    depth = gx_count // 2
    chunks = wbuf.shape[0]
    width = wbuf.shape[2]
    _, _, _, _, half, _ = full.shape
    rows = 2 * depth * 2 * half
    core, far, near, sibling, pair, line = position(gx_count)

    def load(c):
        return pltpu.make_async_copy(
            w_ref.at[pl.ds(pl.multiple_of(c * CHUNK, CHUNK), CHUNK), :], wbuf.at[c], wsem.at[c]
        )

    @pl.loop(0, chunks)
    def _(c):
        load(c).start()

    greet(sibling, pair, line, depth)
    give = remote(
        att_ref.at[1 - core],
        full.at[:, near, far, core],
        gsem.at[0],
        gsem.at[1],
        sibling,
    )
    give.start()

    @pl.loop(0, chunks)
    def _(c):
        full[c, near, far, core] = att_ref[core, c]

    acc[...] = jnp.zeros_like(acc)
    give.wait()

    def along(c, d):
        block = full.at[c, near, far]
        return remote(block, block, zs.at[c, d], zr.at[c, d], line(d))

    def across(c, d):
        block = full.at[c, near, lax.rem(far + depth - d, depth)]
        return remote(block, block, ys.at[c, d], yr.at[c, d], pair)

    @pl.loop(0, chunks)
    def _(c):
        across(c, 0).start()
        for d in range(1, depth):
            along(c, d).start()

    lag = 1

    @pl.loop(0, chunks + lag)
    def _(c):
        @pl.when(c < chunks)
        def _():
            for d in range(1, depth):
                along(c, d).wait_recv()
                across(c, d).start()

        @pl.when(c >= lag)
        def _():
            cc = c - lag
            for d in range(depth):
                across(cc, d).wait_recv()
            load(cc).wait()
            acc[...] += jnp.dot(
                full[cc].reshape(rows, CHUNK), wbuf[cc], preferred_element_type=jnp.float32
            ).reshape(2, depth, 2 * half, width)

    keep = depth // 2
    last = remote(
        acc.at[:, pl.ds((1 - core) * keep, keep)], acc_in, fsem.at[0], fsem.at[1], sibling
    )
    last.start()

    @pl.loop(0, chunks)
    def _(c):
        across(c, 0).wait_send()
        for d in range(1, depth):
            along(c, d).wait_send()
            across(c, d).wait_send()

    last.wait()
    for z in range(keep):
        for y in range(2):
            out_ref[z, y] = (acc[y, core * keep + z] + acc_in[y, z]).astype(out_ref.dtype)


def output(attended, w_out, gx_count):
    _, chunks, half, _ = attended.shape
    width = w_out.shape[1]
    depth = gx_count // 2
    keep = depth // 2
    vmem = pl.BlockSpec(memory_space=pltpu.VMEM)
    dma = pltpu.SemaphoreType.DMA
    return pl.pallas_call(
        functools.partial(output_kernel, gx_count),
        out_shape=jax.ShapeDtypeStruct((keep, 2, 2 * half, width), jnp.bfloat16),
        in_specs=[vmem, pl.BlockSpec(memory_space=pl.ANY)],
        out_specs=vmem,
        scratch_shapes=[
            pltpu.VMEM((chunks, CHUNK, width), jnp.bfloat16),
            pltpu.VMEM((chunks, 2, depth, 2, half, CHUNK), jnp.bfloat16),
            pltpu.VMEM((2, depth, 2 * half, width), jnp.float32),
            pltpu.VMEM((2, keep, 2 * half, width), jnp.float32),
            dma((chunks,)),
            dma((2,)),
            dma((chunks, depth)),
            dma((chunks, depth)),
            dma((chunks, depth)),
            dma((chunks, depth)),
            dma((2,)),
        ],
        compiler_params=pltpu.CompilerParams(
            collective_id=2, has_side_effects=True, vmem_limit_bytes=56 * 1024 * 1024
        ),
    )(attended, w_out)


def attend_kernel(steps, lengths_ref, q_ref, kn_ref, vn_ref, k_ref, v_ref, out_ref):
    live = lengths_ref[pl.program_id(0)]
    total = k_ref.shape[1]
    block = total // 4
    for count in range(1, 5):

        @pl.when((live > (count - 1) * block) & (live <= count * block))
        def _():
            attend_slots(
                steps, count * block, live, q_ref, kn_ref, vn_ref, k_ref, v_ref, out_ref
            )


def attend_slots(steps, slots, live, q_ref, kn_ref, vn_ref, k_ref, v_ref, out_ref):
    kv_heads, queries, head_dim = q_ref.shape[1:]
    inverse = 1.0 / math.sqrt(head_dim)
    mask = lax.broadcasted_iota(jnp.int32, (queries, slots), 1) < live
    step = lax.broadcasted_iota(jnp.int32, (queries, 1), 0) // (queries // steps)
    for g in range(kv_heads):
        cols = slice(g * head_dim, (g + 1) * head_dim)
        q = q_ref[0, g]
        scores = (
            lax.dot_general(
                q, k_ref[0, :slots, cols], (((1,), (1,)), ((), ())), preferred_element_type=jnp.float32
            )
            * inverse
        )
        scores = jnp.where(mask, scores, -jnp.inf)
        wide = q.astype(jnp.float32)
        highest = jnp.max(scores, axis=1, keepdims=True)
        fresh = []
        for s in range(steps):
            one = (
                jnp.sum(wide * kn_ref[0, s : s + 1, cols].astype(jnp.float32), axis=1, keepdims=True)
                * inverse
            )
            one = jnp.where(step >= s, one, -jnp.inf)
            highest = jnp.maximum(highest, one)
            fresh.append(one)
        exp_cache = jnp.exp(scores - highest)
        denominator = jnp.sum(exp_cache, axis=1, keepdims=True)
        exp_new = [jnp.exp(one - highest) for one in fresh]
        for one in exp_new:
            denominator = denominator + one
        scale = 1.0 / denominator
        weights = (exp_cache * scale).astype(jnp.bfloat16)
        result = jnp.dot(weights, v_ref[0, :slots, cols], preferred_element_type=jnp.float32)
        for s in range(steps):
            weight = (exp_new[s] * scale).astype(jnp.bfloat16).astype(jnp.float32)
            result = result + weight * vn_ref[0, s : s + 1, cols].astype(jnp.float32)
        out_ref[0, g] = result.astype(jnp.bfloat16)


def attend(lengths, queries, keys_new, values_new, keys, values):
    rows, kv_heads, count, head_dim = queries.shape
    steps = keys_new.shape[1]
    slots, width = keys.shape[1:]
    return pl.pallas_call(
        functools.partial(attend_kernel, steps),
        out_shape=jax.ShapeDtypeStruct(queries.shape, jnp.bfloat16),
        grid_spec=pltpu.PrefetchScalarGridSpec(
            num_scalar_prefetch=1,
            grid=(rows,),
            in_specs=[
                pl.BlockSpec((1, kv_heads, count, head_dim), lambda r, _: (r, 0, 0, 0)),
                pl.BlockSpec((1, steps, width), lambda r, _: (r, 0, 0)),
                pl.BlockSpec((1, steps, width), lambda r, _: (r, 0, 0)),
                pl.BlockSpec((1, slots, width), lambda r, _: (r, 0, 0)),
                pl.BlockSpec((1, slots, width), lambda r, _: (r, 0, 0)),
            ],
            out_specs=pl.BlockSpec((1, kv_heads, count, head_dim), lambda r, _: (r, 0, 0, 0)),
        ),
        compiler_params=pltpu.CompilerParams(vmem_limit_bytes=56 * 1024 * 1024),
    )(lengths, queries, keys_new, values_new, keys, values)


def rotary_embed(inputs, token_positions):
    half_dim = inputs.shape[-1] // 2
    frequency = rope_base ** (-jnp.arange(half_dim, dtype=jnp.float32) / half_dim)
    angles = token_positions.astype(jnp.float32)[..., None, None] * frequency
    cosine = jnp.cos(angles)
    sine_part = jnp.sin(angles)
    lower_half = inputs[..., :half_dim]
    upper_half = inputs[..., half_dim:]
    return jnp.concatenate(
        [
            lower_half * cosine - upper_half * sine_part,
            upper_half * cosine + lower_half * sine_part,
        ],
        axis=-1,
    )


def local(
    hidden,
    norm_gain,
    w_query,
    key_weight,
    value_weight,
    w_out,
    stored_rotated_keys,
    stored_value_rows,
    lengths,
):
    gx_count = lax.axis_size("gx")
    gy_count = lax.axis_size("gy")
    steps, width = hidden.shape[1:]
    head_dim = HEAD_SIZE
    local_rows = lengths.shape[0]
    key_width = key_weight.shape[1]
    kv_heads = key_width * gy_count // head_dim
    mixed = project(
        hidden.reshape(-1, width),
        norm_gain.reshape(1, width),
        w_query,
        key_weight,
        value_weight,
        gx_count,
    )
    query_part = mixed[:, :-1]
    chunks = query_part.shape[1]
    per_chunk = CHUNK // head_dim
    queries = query_part.reshape(gy_count, chunks, local_rows, steps, per_chunk, head_dim)
    queries = queries.transpose(2, 3, 0, 1, 4, 5).reshape(local_rows, steps, -1, head_dim)
    fresh = mixed[:, -1].reshape(gy_count, local_rows, steps, 2, key_width).transpose(1, 2, 3, 0, 4)
    keys_new = fresh[:, :, 0].reshape(local_rows, steps, -1, head_dim)
    values_new = fresh[:, :, 1].reshape(local_rows, steps, -1)
    token_positions = lengths[:, None] + jnp.arange(steps)
    queries = rotary_embed(queries.astype(jnp.float32), token_positions).astype(jnp.bfloat16)
    keys_new = rotary_embed(keys_new.astype(jnp.float32), token_positions).astype(jnp.bfloat16)
    per_group = queries.shape[2] // kv_heads
    queries = queries.reshape(local_rows, steps, kv_heads, per_group, head_dim)
    queries = queries.transpose(0, 2, 1, 3, 4).reshape(
        local_rows, kv_heads, steps * per_group, head_dim
    )
    attended = attend(
        lengths,
        queries,
        keys_new.reshape(local_rows, steps, -1),
        values_new,
        stored_rotated_keys,
        stored_value_rows,
    )
    attended = attended.reshape(local_rows, gy_count, -1, steps, per_group // per_chunk, CHUNK)
    attended = attended.transpose(1, 2, 4, 0, 3, 5).reshape(
        gy_count, chunks, local_rows * steps, CHUNK
    )
    result = output(attended, w_out, gx_count)
    return result.reshape(-1, steps, width)


def solution(mesh):
    return jax.shard_map(
        local,
        mesh=mesh,
        in_specs=(
            P(("groups", "gy"), None, "gx"),
            P("gx"),
            P("gx", "gy"),
            P("gx", "gy"),
            P("gx", "gy"),
            P("gy", "gx"),
            P(("groups", "gx", "gy"), None, None),
            P(("groups", "gx", "gy"), None, None),
            P(("groups", "gx", "gy")),
        ),
        out_specs=P(("groups", "gy"), None, "gx"),
        check_vma=False,
    )
```

time: 319 us -> 118 us (0.37)
  waiting for transfers between devices: 190 us -> 0 us
  Pallas kernels: 0 us -> 104 us
  matrix products: 54.3 us -> 0 us
  blocking collectives: 44.3 us -> 0 us
  between operations: 13.9 us -> 0.14 us
  other arithmetic: 10.6 us -> 2.36 us
  local copies, waits for them, and re-layouts: 5.35 us -> 10.8 us
    reduce_scatter x4 -> x0, waiting for transfers between devices: 130 us -> none  [the longest x2 119 us: local(): lax.psum_scatter(jnp.concatenate([jnp.dot(flat_rows, w_query, preferred_e...]
    pallas_call x0 -> x3, Pallas kernels: none -> 104 us  [the longest x1 48.7 us: project(): pl.pallas_call(functools.partial(project_kernel, gx_count, rows_block), o...]
    all_gather x2 -> x0, waiting for transfers between devices: 60 us -> none  [local(): lax.all_gather(returned, 'gx', axis=0, tiled=True)]
    dot_general x15 -> x0, matrix products: 54.3 us -> none  [the longest x2 18.9 us: local(): jnp.dot(lax.all_gather(returned, 'gx', axis=0, tiled=True), w_out, prefer...]
    psum x1 -> x0, blocking collectives: 23.3 us -> none  [local(): row_sumsq = lax.psum(partial_sq, 'gx')]
    all_to_all x4 -> x0, blocking collectives: 16.7 us -> none  [the longest x2 9.06 us: local(): lax.all_to_all(blocks, 'gy', split_axis=1, concat_axis=0, tiled=True)]
    reshape x6, local copies, waits for them, and re-layouts: 0.27 us -> 7.57 us  [the longest x1 2.17 us: local(): return result.reshape(-1, steps, width)]
    all_gather x2 -> x0, blocking collectives: 4.36 us -> none  [local(): gathered = lax.all_gather(normed, 'gy', axis=0, tiled=True)]
  transfers between devices with their start and end apart: 6 -> 0, of which waited for: 5 -> 0; matrix products, arithmetic and copies ran while one was open for 12% -> 0% of each run, Pallas kernels for 0% -> 0%
where the time goes in v1:
time: 118 us; the launch traced here: 117 us
  Pallas kernels  104 us (88%)
  local copies, waits for them, and re-layouts  10.8 us (9%)
  other arithmetic  2.36 us (2%)
    pallas_call x1, Pallas kernels, project(): pl.pallas_call(functools.partial(project_kernel, gx_count, rows_block), o...  48.7 us
    pallas_call x1, Pallas kernels, output(): pl.pallas_call(functools.partial(output_kernel, gx_count), out_shape=jax....  38.9 us
    pallas_call x1, Pallas kernels, attend(): pl.pallas_call(functools.partial(attend_kernel, steps), out_shape=jax.Sha...  16.1 us

profile of v1, /device:TPU:0, one launch (start us, length us, event | category | flops | bytes accessed | tf_op | source)
XLA Modules:
  0.0 117.0 jit_solution(6234056406385260120)
XLA Ops:
  0.0 0.7 add_convert_fusion.2
  0.7 1.3 %reshape.73.gain_ref = bf16[1,2048]{1,0:T(2,128)(2,1)} reshape(bf16[2048]{0:T(1024)(128)(2,1)} %param.10) | data formatting | bytes 8192 | tf_op jit(solution)/shard_map/reshape | solution.py:530
  2.0 0.1 multiply_cosine_fusion
  2.1 2.0 %reshape.72.x_ref = bf16[128,2048]{1,0:T(8,128)(2,1)} reshape(bf16[64,2,2048]{2,1,0:T(2,128)(2,1)} %param.9) | data formatting | bytes 1048576 | tf_op jit(solution)/shard_map/reshape | solution.py:529
  4.1 48.7 %shard_map.91 = bf16[2,9,16,512]{3,2,1,0:T(8,128)(2,1)} custom-call(bf16[128,2048]{1,0:T(8,128)(2,1)} %reshape.72.x_ref, bf16[1,2048]{1,0:T(2,128)(2,1)} %reshape.73.gain_ref, bf16[2048,4096]{1,0:T(8,128)(2,1)} %wq_ref.1, bf16[2048,256]{1,0:T(8,128)(2,1)} %kw_ref.1, bf16[2048,256]{1,0:T(8,128)(2,1)} %vw_ref.1), custom_call_target="tpu_custom_call" | custom-call | tf_op jit(solution)/shard_map/pallas_call | solution.py:247
  52.9 0.8 slice.27
  53.7 0.6 reshape_squeeze.8.vn_ref
  54.4 0.1 subtract_convert_fusion.1
  54.5 0.1 pad_maximum_fusion
  54.6 0.6 convert_element_type.40.kn_ref
  55.2 1.0 slice_convert_fusion
  56.2 0.2 reshape.80
  56.4 0.1 copy.12
  56.5 0.2 subtract_convert_fusion
  56.8 0.2 maximum_bitcast_fusion
  57.0 0.7 copy.15
  57.7 16.1 %shard_map.92 = bf16[8,4,32,128]{3,2,1,0:T(8,128)(2,1)} custom-call(s32[8]{0:T(128)} %lengths_ref.1, bf16[8,4,32,128]{3,2,1,0:T(8,128)(2,1)} %bitcast.27, bf16[8,2,512]{2,1,0:T(2,128)(2,1)} %convert_element_type.40.kn_ref, bf16[8,2,512]{2,1,0:T(2,128)(2,1)} %reshape_squeeze.8.vn_ref, bf16[8,1024,512]{2,1,0:T(8,128)(2,1)} %k_ref.1, bf16[8,1024,512]{2,1,0:T(8,128)(2,1)} %v_ref.1), custom_call_target="tpu_custom_call" | custom-call | tf_op jit(solution)/shard_map/pallas_call | solution.py:474
  73.9 1.1 reshape.75
  74.9 0.2 copy.22
  75.2 0.8 reshape.76.att_ref
  76.0 38.9 %shard_map.93 = bf16[2,2,32,2048]{3,2,1,0:T(8,128)(2,1)} custom-call(bf16[2,8,16,512]{3,2,1,0:T(8,128)(2,1)} %reshape.76.att_ref, bf16[4096,2048]{1,0:T(8,128)(2,1)} %w_ref.1), custom_call_target="tpu_custom_call" | custom-call | tf_op jit(solution)/shard_map/pallas_call | solution.py:393
  114.8 2.2 %reshape.77 = bf16[64,2,2048]{2,1,0:T(2,128)(2,1)} reshape(bf16[2,2,32,2048]{3,2,1,0:T(8,128)(2,1)} %shard_map.93) | data formatting | bytes 1048576 | tf_op jit(solution)/shard_map/reshape | solution.py:565
  (9 shorter events, 0.2 us)

commit v2 on v1

--- a/solution.py
+++ b/solution.py
@@ -74,6 +74,7 @@
     out_ref,
     wbuf,
     xs,
+    sums,
     mine,
     mid,
     pair_sums,
@@ -128,14 +129,16 @@
     send_x = remote(x_ref, xs.at[core], xsem.at[0], xsem.at[1], sibling)
     send_x.start()
     xs[core] = x_ref[...]
+
+    def row_sums(g):
+        wide = xs[g].astype(jnp.float32)
+        column = jnp.sum(wide * wide, axis=1, keepdims=True)
+        sums[g] = jnp.transpose(jnp.broadcast_to(column, (half_rows, 128)))[0:8, :]
+
+    row_sums(core)
     send_x.wait()
-
-    columns = []
-    for g in range(2):
-        wide = xs[g].astype(jnp.float32)
-        columns.append(jnp.sum(wide * wide, axis=1, keepdims=True))
-    column = jnp.concatenate(columns, axis=0)
-    mine[...] = jnp.transpose(jnp.broadcast_to(column, (rows, 128)))[0:8, :]
+    row_sums(1 - core)
+    mine[...] = jnp.concatenate([sums[0], sums[1]], axis=1)
     swap = remote(mine, pair_sums, psem.at[0], psem.at[1], pair)
     swap.start()
     swap.wait()
@@ -252,6 +255,7 @@
         scratch_shapes=[
             pltpu.VMEM((chunks, width, CHUNK), jnp.bfloat16),
             pltpu.VMEM((2, half_rows, width), jnp.bfloat16),
+            pltpu.VMEM((2, 8, half_rows), jnp.float32),
             pltpu.VMEM((8, rows), jnp.float32),
             pltpu.VMEM((8, rows), jnp.float32),
             pltpu.VMEM((8, rows), jnp.float32),
@@ -338,21 +342,22 @@
         block = full.at[c, near, lax.rem(far + depth - d, depth)]
         return remote(block, block, ys.at[c, d], yr.at[c, d], pair)
 
-    @pl.loop(0, chunks)
-    def _(c):
-        across(c, 0).start()
-        for d in range(1, depth):
-            along(c, d).start()
-
-    lag = 1
+    ahead = 2
+    lag = ahead + 1
 
     @pl.loop(0, chunks + lag)
     def _(c):
         @pl.when(c < chunks)
         def _():
+            for d in range(depth - 1, 0, -1):
+                along(c, d).start()
+            across(c, 0).start()
+
+        @pl.when((c >= ahead) & (c < chunks + ahead))
+        def _():
             for d in range(1, depth):
-                along(c, d).wait_recv()
-                across(c, d).start()
+                along(c - ahead, d).wait_recv()
+                across(c - ahead, d).start()
 
         @pl.when(c >= lag)
         def _():
@@ -432,38 +437,50 @@
     inverse = 1.0 / math.sqrt(head_dim)
     mask = lax.broadcasted_iota(jnp.int32, (queries, slots), 1) < live
     step = lax.broadcasted_iota(jnp.int32, (queries, 1), 0) // (queries // steps)
-    for g in range(kv_heads):
-        cols = slice(g * head_dim, (g + 1) * head_dim)
-        q = q_ref[0, g]
-        scores = (
-            lax.dot_general(
-                q, k_ref[0, :slots, cols], (((1,), (1,)), ((), ())), preferred_element_type=jnp.float32
+    heads = [slice(g * head_dim, (g + 1) * head_dim) for g in range(kv_heads)]
+    mask = jnp.concatenate([mask] * kv_heads, axis=0)
+    scores = [
+        lax.dot_general(
+            q_ref[0, g],
+            k_ref[0, :slots, cols],
+            (((1,), (1,)), ((), ())),
+            preferred_element_type=jnp.float32,
+        )
+        for g, cols in enumerate(heads)
+    ]
+    scores = jnp.where(mask, jnp.concatenate(scores, axis=0) * inverse, -jnp.inf)
+    highest = jnp.max(scores, axis=1, keepdims=True)
+    fresh = []
+    for s in range(steps):
+        one = [
+            jnp.sum(
+                q_ref[0, g].astype(jnp.float32) * kn_ref[0, s : s + 1, cols].astype(jnp.float32),
+                axis=1,
+                keepdims=True,
             )
             * inverse
+            for g, cols in enumerate(heads)
+        ]
+        one = jnp.concatenate([jnp.where(step >= s, part, -jnp.inf) for part in one], axis=0)
+        highest = jnp.maximum(highest, one)
+        fresh.append(one)
+    exp_cache = jnp.exp(scores - highest)
+    denominator = jnp.sum(exp_cache, axis=1, keepdims=True)
+    exp_new = [jnp.exp(one - highest) for one in fresh]
+    for one in exp_new:
+        denominator = denominator + one
+    scale = 1.0 / denominator
+    weights = (exp_cache * scale).astype(jnp.bfloat16)
+    new_weights = [(one * scale).astype(jnp.bfloat16).astype(jnp.float32) for one in exp_new]
+    for g, cols in enumerate(heads):
+        rows = slice(g * queries, (g + 1) * queries)
+        result = jnp.dot(
+            weights[rows, :], v_ref[0, :slots, cols], preferred_element_type=jnp.float32
         )
-        scores = jnp.where(mask, scores, -jnp.inf)
-        wide = q.astype(jnp.float32)
-        highest = jnp.max(scores, axis=1, keepdims=True)
-        fresh = []
         for s in range(steps):
-            one = (
-                jnp.sum(wide * kn_ref[0, s : s + 1, cols].astype(jnp.float32), axis=1, keepdims=True)
-                * inverse
+            result = result + new_weights[s][rows, :] * vn_ref[0, s : s + 1, cols].astype(
+                jnp.float32
             )
-            one = jnp.where(step >= s, one, -jnp.inf)
-            highest = jnp.maximum(highest, one)
-            fresh.append(one)
-        exp_cache = jnp.exp(scores - highest)
-        denominator = jnp.sum(exp_cache, axis=1, keepdims=True)
-        exp_new = [jnp.exp(one - highest) for one in fresh]
-        for one in exp_new:
-            denominator = denominator + one
-        scale = 1.0 / denominator
-        weights = (exp_cache * scale).astype(jnp.bfloat16)
-        result = jnp.dot(weights, v_ref[0, :slots, cols], preferred_element_type=jnp.float32)
-        for s in range(steps):
-            weight = (exp_new[s] * scale).astype(jnp.bfloat16).astype(jnp.float32)
-            result = result + weight * vn_ref[0, s : s + 1, cols].astype(jnp.float32)
         out_ref[0, g] = result.astype(jnp.bfloat16)
 
 

time: 118 us -> 114 us (0.966)
  Pallas kernels: 104 us -> 99.9 us
    pallas_call x1, Pallas kernels: 16.1 us -> 12.3 us  [attend(): pl.pallas_call(functools.partial(attend_kernel, steps), out_shape=jax.Sha...]
where the time goes in v2:
time: 114 us; the launch traced here: 113 us
  Pallas kernels  99.9 us (88%)
  local copies, waits for them, and re-layouts  10.8 us (9%)
  other arithmetic  2.36 us (2%)
    pallas_call x1, Pallas kernels, project(): pl.pallas_call(functools.partial(project_kernel, gx_count, rows_block), o...  48.5 us
    pallas_call x1, Pallas kernels, output(): pl.pallas_call(functools.partial(output_kernel, gx_count), out_shape=jax....  39 us
    pallas_call x1, Pallas kernels, attend(): pl.pallas_call(functools.partial(attend_kernel, steps), out_shape=jax.Sha...  12.3 us

profile of v2, /device:TPU:0, one launch (start us, length us, event | category | flops | bytes accessed | tf_op | source)
XLA Modules:
  0.0 113.1 jit_solution(14790811773881700675)
XLA Ops:
  0.0 0.7 add_convert_fusion.2
  0.7 1.3 %reshape.73.gain_ref = bf16[1,2048]{1,0:T(2,128)(2,1)} reshape(bf16[2048]{0:T(1024)(128)(2,1)} %param.10) | data formatting | bytes 8192 | tf_op jit(solution)/shard_map/reshape | solution.py:547
  2.0 0.1 multiply_cosine_fusion
  2.1 2.0 %reshape.72.x_ref = bf16[128,2048]{1,0:T(8,128)(2,1)} reshape(bf16[64,2,2048]{2,1,0:T(2,128)(2,1)} %param.9) | data formatting | bytes 1048576 | tf_op jit(solution)/shard_map/reshape | solution.py:546
  4.1 48.5 %shard_map.91 = bf16[2,9,16,512]{3,2,1,0:T(8,128)(2,1)} custom-call(bf16[128,2048]{1,0:T(8,128)(2,1)} %reshape.72.x_ref, bf16[1,2048]{1,0:T(2,128)(2,1)} %reshape.73.gain_ref, bf16[2048,4096]{1,0:T(8,128)(2,1)} %wq_ref.1, bf16[2048,256]{1,0:T(8,128)(2,1)} %kw_ref.1, bf16[2048,256]{1,0:T(8,128)(2,1)} %vw_ref.1), custom_call_target="tpu_custom_call" | custom-call | tf_op jit(solution)/shard_map/pallas_call | solution.py:250
  52.7 0.8 slice.27
  53.6 0.6 reshape_squeeze.8.vn_ref
  54.2 0.1 subtract_convert_fusion.1
  54.3 0.1 pad_maximum_fusion
  54.4 0.6 convert_element_type.40.kn_ref
  55.0 1.0 slice_convert_fusion
  56.0 0.2 reshape.80
  56.2 0.1 copy.12
  56.3 0.2 subtract_convert_fusion
  56.7 0.2 maximum_bitcast_fusion
  56.8 0.7 copy.15
  57.5 12.3 %shard_map.92 = bf16[8,4,32,128]{3,2,1,0:T(8,128)(2,1)} custom-call(s32[8]{0:T(128)} %lengths_ref.1, bf16[8,4,32,128]{3,2,1,0:T(8,128)(2,1)} %bitcast.27, bf16[8,2,512]{2,1,0:T(2,128)(2,1)} %convert_element_type.40.kn_ref, bf16[8,2,512]{2,1,0:T(2,128)(2,1)} %reshape_squeeze.8.vn_ref, bf16[8,1024,512]{2,1,0:T(8,128)(2,1)} %k_ref.1, bf16[8,1024,512]{2,1,0:T(8,128)(2,1)} %v_ref.1), custom_call_target="tpu_custom_call" | custom-call | tf_op jit(solution)/shard_map/pallas_call | solution.py:491
  69.9 1.1 reshape.75
  70.9 0.2 copy.22
  71.1 0.8 reshape.76.att_ref
  71.9 39.0 %shard_map.93 = bf16[2,2,32,2048]{3,2,1,0:T(8,128)(2,1)} custom-call(bf16[2,8,16,512]{3,2,1,0:T(8,128)(2,1)} %reshape.76.att_ref, bf16[4096,2048]{1,0:T(8,128)(2,1)} %w_ref.1), custom_call_target="tpu_custom_call" | custom-call | tf_op jit(solution)/shard_map/pallas_call | solution.py:398
  111.0 2.2 %reshape.77 = bf16[64,2,2048]{2,1,0:T(2,128)(2,1)} reshape(bf16[2,2,32,2048]{3,2,1,0:T(8,128)(2,1)} %shard_map.93) | data formatting | bytes 1048576 | tf_op jit(solution)/shard_map/reshape | solution.py:582
  (9 shorter events, 0.2 us)

commit v3 on v2

--- a/solution.py
+++ b/solution.py
@@ -10,6 +10,7 @@
 
 HEAD_SIZE = 128
 CHUNK = 512
+OUT_CHUNK = 1024
 WIRE = jnp.int16
 SMALL = 2.0**-20
 CODES = 32767.0 / math.log(2.0**34.5)
@@ -310,7 +311,7 @@
 
     def load(c):
         return pltpu.make_async_copy(
-            w_ref.at[pl.ds(pl.multiple_of(c * CHUNK, CHUNK), CHUNK), :], wbuf.at[c], wsem.at[c]
+            w_ref.at[pl.ds(pl.multiple_of(c * OUT_CHUNK, OUT_CHUNK), OUT_CHUNK), :], wbuf.at[c], wsem.at[c]
         )
 
     @pl.loop(0, chunks)
@@ -342,7 +343,7 @@
         block = full.at[c, near, lax.rem(far + depth - d, depth)]
         return remote(block, block, ys.at[c, d], yr.at[c, d], pair)
 
-    ahead = 2
+    ahead = 1
     lag = ahead + 1
 
     @pl.loop(0, chunks + lag)
@@ -366,7 +367,7 @@
                 across(cc, d).wait_recv()
             load(cc).wait()
             acc[...] += jnp.dot(
-                full[cc].reshape(rows, CHUNK), wbuf[cc], preferred_element_type=jnp.float32
+                full[cc].reshape(rows, OUT_CHUNK), wbuf[cc], preferred_element_type=jnp.float32
             ).reshape(2, depth, 2 * half, width)
 
     keep = depth // 2
@@ -401,8 +402,8 @@
         in_specs=[vmem, pl.BlockSpec(memory_space=pl.ANY)],
         out_specs=vmem,
         scratch_shapes=[
-            pltpu.VMEM((chunks, CHUNK, width), jnp.bfloat16),
-            pltpu.VMEM((chunks, 2, depth, 2, half, CHUNK), jnp.bfloat16),
+            pltpu.VMEM((chunks, OUT_CHUNK, width), jnp.bfloat16),
+            pltpu.VMEM((chunks, 2, depth, 2, half, OUT_CHUNK), jnp.bfloat16),
             pltpu.VMEM((2, depth, 2 * half, width), jnp.float32),
             pltpu.VMEM((2, keep, 2 * half, width), jnp.float32),
             dma((chunks,)),
@@ -574,9 +575,9 @@
         stored_rotated_keys,
         stored_value_rows,
     )
-    attended = attended.reshape(local_rows, gy_count, -1, steps, per_group // per_chunk, CHUNK)
+    attended = attended.reshape(local_rows, gy_count, -1, steps, per_group * head_dim // OUT_CHUNK, OUT_CHUNK)
     attended = attended.transpose(1, 2, 4, 0, 3, 5).reshape(
-        gy_count, chunks, local_rows * steps, CHUNK
+        gy_count, -1, local_rows * steps, OUT_CHUNK
     )
     result = output(attended, w_out, gx_count)
     return result.reshape(-1, steps, width)

time: 114 us -> 114 us (level)
  no operation moved by 1% of the time
where the time goes in v3:
time: 114 us; the launch traced here: 113 us
  Pallas kernels  99.7 us (87%)
  local copies, waits for them, and re-layouts  10.7 us (9%)
  other arithmetic  2.36 us (2%)
    pallas_call x1, Pallas kernels, project(): pl.pallas_call(functools.partial(project_kernel, gx_count, rows_block), o...  48.5 us
    pallas_call x1, Pallas kernels, output(): pl.pallas_call(functools.partial(output_kernel, gx_count), out_shape=jax....  39.3 us
    pallas_call x1, Pallas kernels, attend(): pl.pallas_call(functools.partial(attend_kernel, steps), out_shape=jax.Sha...  11.9 us

profile of v3, /device:TPU:0, one launch (start us, length us, event | category | flops | bytes accessed | tf_op | source)
XLA Modules:
  0.0 112.9 jit_solution(9654599808194943785)
XLA Ops:
  0.0 0.7 add_convert_fusion.2
  0.7 1.3 %reshape.73.gain_ref = bf16[1,2048]{1,0:T(2,128)(2,1)} reshape(bf16[2048]{0:T(1024)(128)(2,1)} %param.10) | data formatting | bytes 8192 | tf_op jit(solution)/shard_map/reshape | solution.py:548
  2.0 0.1 multiply_cosine_fusion
  2.1 2.0 %reshape.72.x_ref = bf16[128,2048]{1,0:T(8,128)(2,1)} reshape(bf16[64,2,2048]{2,1,0:T(2,128)(2,1)} %param.9) | data formatting | bytes 1048576 | tf_op jit(solution)/shard_map/reshape | solution.py:547
  4.1 48.5 %shard_map.91 = bf16[2,9,16,512]{3,2,1,0:T(8,128)(2,1)} custom-call(bf16[128,2048]{1,0:T(8,128)(2,1)} %reshape.72.x_ref, bf16[1,2048]{1,0:T(2,128)(2,1)} %reshape.73.gain_ref, bf16[2048,4096]{1,0:T(8,128)(2,1)} %wq_ref.1, bf16[2048,256]{1,0:T(8,128)(2,1)} %kw_ref.1, bf16[2048,256]{1,0:T(8,128)(2,1)} %vw_ref.1), custom_call_target="tpu_custom_call" | custom-call | tf_op jit(solution)/shard_map/pallas_call | solution.py:251
  52.7 0.8 slice.27
  53.6 0.6 reshape_squeeze.8.vn_ref
  54.2 0.1 subtract_convert_fusion.1
  54.3 0.1 pad_maximum_fusion
  54.4 0.6 convert_element_type.40.kn_ref
  55.0 1.0 slice_convert_fusion
  56.0 0.2 reshape.80
  56.2 0.1 copy.12
  56.3 0.2 subtract_convert_fusion
  56.7 0.2 maximum_bitcast_fusion
  56.8 0.7 copy.15
  57.5 11.9 %shard_map.92 = bf16[8,4,32,128]{3,2,1,0:T(8,128)(2,1)} custom-call(s32[8]{0:T(128)} %lengths_ref.1, bf16[8,4,32,128]{3,2,1,0:T(8,128)(2,1)} %bitcast.27, bf16[8,2,512]{2,1,0:T(2,128)(2,1)} %convert_element_type.40.kn_ref, bf16[8,2,512]{2,1,0:T(2,128)(2,1)} %reshape_squeeze.8.vn_ref, bf16[8,1024,512]{2,1,0:T(8,128)(2,1)} %k_ref.1, bf16[8,1024,512]{2,1,0:T(8,128)(2,1)} %v_ref.1), custom_call_target="tpu_custom_call" | custom-call | tf_op jit(solution)/shard_map/pallas_call | solution.py:492
  69.4 1.0 reshape.75
  70.5 0.2 copy.22
  70.7 0.8 reshape.76.att_ref
  71.5 39.3 %shard_map.93 = bf16[2,2,32,2048]{3,2,1,0:T(8,128)(2,1)} custom-call(bf16[2,4,16,1024]{3,2,1,0:T(8,128)(2,1)} %reshape.76.att_ref, bf16[4096,2048]{1,0:T(8,128)(2,1)} %w_ref.1), custom_call_target="tpu_custom_call" | custom-call | tf_op jit(solution)/shard_map/pallas_call | solution.py:399
  110.8 2.2 %reshape.77 = bf16[64,2,2048]{2,1,0:T(2,128)(2,1)} reshape(bf16[2,2,32,2048]{3,2,1,0:T(8,128)(2,1)} %shard_map.93) | data formatting | bytes 1048576 | tf_op jit(solution)/shard_map/reshape | solution.py:583
  (9 shorter events, 0.2 us)
